TPU v7x, 512 devices: a whole 4x4x16 slice. The times are simulated.
512 devices in a mesh: pm: 2 (over y_lo), ka: 128 (over x, z, core), isdf: 2 (over y_hi).
Axes of the slice: x: 4, y: 4 (y_hi: 2, y_lo: 2; y = y_hi * 2 + y_lo), z: 16, core: 2. Of those that a mesh axis runs over, the one named last changes fastest.
Arguments:
- amplitudes: bfloat16 [2, 2, 2, 256, 64, 256], P('pm', None, None, 'ka'), may hold values from -6 to 6
- conduction: bfloat16 [2, 256, 256, 512], P(None, 'ka', None, 'isdf'), may hold values from -0.375 to 0.375
- valence: bfloat16 [2, 256, 64, 512], P(None, 'ka'), may hold values from -0.75 to 0.75
- energy: float32 [256, 64, 256], P('ka', None, 'isdf'), may hold values from 0.5 to 2.5
- screened: bfloat16 [4, 2, 512, 512], P(None, None, 'isdf'), may hold values from -0.59765625 to 0.59765625
- coulomb: float32 [512, 512], P(None, 'isdf'), may hold values from -0.03125 to 0.03125
- mirror: int32 [256], P('ka'), may hold values from 0 to 255, as said below
- transfer_class: int32 [256, 256], P('ka'), may hold values from 0 to 3, as said below
Outputs:
- response: bfloat16 [2, 2, 2, 256, 64, 256], P('pm', None, None, 'ka', None, 'isdf')
Inputs may be any that keep to these rules, and one draw needn't show every extreme that they name: mirror[mirror[k]] = k; a k-point of block j (the aligned block of 2 k-points that holds it) has its mirror in block 127 - j. transfer_class[k, k2] depends only on (k - k2) mod 256.
All inputs are finite; a program needn't handle non-finite values.
Results may differ from a plain program's by a relative error of at most 0.015.
Values may be sent and summed in bfloat16 or wider, within the bound.
A program may use at most 128 MiB of HBM per device.

v0:
```python
import jax
import jax.numpy as jnp
from jax import lax
from jax.sharding import PartitionSpec as P

REACH = 2
HIGHEST = lax.Precision.HIGHEST


def swapped(block, axis, apart):
    count = lax.axis_size(axis)
    route = []
    for low in range(count):
        high = low | 1 << apart
        if high != low and high < count:
            route += [(low, high), (high, low)]
    return lax.ppermute(block, axis, route)


def shifted(value, axis, by):
    size = lax.axis_size(axis)
    return lax.ppermute(value, axis, [(i, (i + by) % size) for i in range(size)])


def pair_einsum(pattern, left, right, conjugate):

    def single(first, second):
        return jnp.einsum(pattern, first, second, preferred_element_type=jnp.float32)

    if conjugate:
        real_part = single(left[0], right[0]) + single(left[1], right[1])
        imag_part = single(left[1], right[0]) - single(left[0], right[1])
    else:
        real_part = single(left[0], right[0]) - single(left[1], right[1])
        imag_part = single(left[0], right[1]) + single(left[1], right[0])
    return (real_part, imag_part)


def conjugated(field):
    return jnp.stack([field[:, 0], -field[:, 1]], axis=1)


def coefficients(vector, conduction):
    real_part, imag_part = pair_einsum(
        "bkvc,kcm->bkvm", (vector[:, 0], vector[:, 1]), (conduction[0], conduction[1]), False
    )
    return jnp.stack([real_part, imag_part], axis=1).astype(jnp.bfloat16)


def amp_bits(field):
    for bit_number in range(lax.axis_size("ka").bit_length() - 1):
        field = swapped(field, "ka", bit_number)
    return field


def result_bits(field):
    for bit_number in range(lax.axis_size("ka").bit_length() - 1):
        field = swapped(field, "ka", bit_number)
    return field


def per_device(amplitudes, conduction, valence, energy, screened, coulomb, mirror, transfer_class):
    pm_index = lax.axis_index("pm")
    ka_index = lax.axis_index("ka")
    isdf_index = lax.axis_index("isdf")
    ka_count = lax.axis_size("ka")
    kpoint_count = conduction.shape[1]
    mu_count = conduction.shape[3]
    point_count = valence.shape[3]
    cond_share = energy.shape[2]
    vector_count = amplitudes.shape[1]
    is_plus = pm_index == 0
    parity = jnp.where(is_plus, 1.0, -1.0).astype(jnp.float32)
    exchange_weight = jnp.where(is_plus, 4.0, 0.0).astype(jnp.float32)
    local_amps = amplitudes[0]
    partner_amps = swapped(local_amps, "pm", 0)
    partner_side = jnp.where(is_plus, partner_amps, local_amps)
    distant_side = amp_bits(partner_side)
    direct = jnp.where(is_plus, local_amps, partner_amps).astype(jnp.float32)
    local_mirror = mirror - (ka_count - 1 - ka_index) * kpoint_count
    flipped = conjugated(jnp.take(distant_side, local_mirror, axis=2).astype(jnp.float32))
    vector = (direct + parity * flipped).astype(jnp.bfloat16)
    own_coef = coefficients(vector, conduction)
    valence_part = lax.dynamic_slice_in_dim(valence, isdf_index * mu_count, mu_count, 3)
    rho_real = jnp.einsum(
        "kvm,bkvm->bm", valence_part[0], own_coef[:, 0], preferred_element_type=jnp.float32
    )
    rho_real = rho_real + jnp.einsum(
        "kvm,bkvm->bm", valence_part[1], own_coef[:, 1], preferred_element_type=jnp.float32
    )
    rho_imag = jnp.einsum(
        "kvm,bkvm->bm", valence_part[0], own_coef[:, 1], preferred_element_type=jnp.float32
    )
    rho_imag = rho_imag - jnp.einsum(
        "kvm,bkvm->bm", valence_part[1], own_coef[:, 0], preferred_element_type=jnp.float32
    )
    density = jnp.stack([rho_real, rho_imag], axis=1)
    spread = jnp.einsum("nm,brm->brn", coulomb, density, precision=HIGHEST)
    spread = lax.psum(spread, ("ka", "isdf"))
    potential = lax.dynamic_slice_in_dim(spread, isdf_index * mu_count, mu_count, 2)
    class_ids = jnp.arange(screened.shape[0], dtype=jnp.int32)

    def accumulate(totals, coef_block, valence_block, source):
        pair_real, pair_imag = pair_einsum(
            "bqvm,qvn->bqmn",
            (coef_block[:, 0], coef_block[:, 1]),
            (valence_block[0], valence_block[1]),
            True,
        )
        pair_real = pair_real.astype(jnp.bfloat16)
        pair_imag = pair_imag.astype(jnp.bfloat16)
        classes = lax.dynamic_slice_in_dim(transfer_class, source * kpoint_count, kpoint_count, 1)
        selector = (classes[:, :, None] == class_ids).astype(jnp.bfloat16)
        total_real, total_imag = totals
        for visitor in range(kpoint_count):
            chosen = jnp.einsum(
                "kw,wrmn->rkmn", selector[:, visitor], screened, preferred_element_type=jnp.float32
            ).astype(jnp.bfloat16)
            screen_real = chosen[0][None].astype(jnp.float32)
            screen_imag = chosen[1][None].astype(jnp.float32)
            visit_real = pair_real[:, visitor][:, None].astype(jnp.float32)
            visit_imag = pair_imag[:, visitor][:, None].astype(jnp.float32)
            total_real = total_real + (screen_real * visit_real - screen_imag * visit_imag)
            total_imag = total_imag + (screen_real * visit_imag + screen_imag * visit_real)
        return (total_real, total_imag)

    payload = (vector, conduction, valence)

    def advance(moving, offset):
        return shifted((moving[0], moving[1], moving[2]), "ka", offset)

    def unpack(moving):
        return (coefficients(moving[0], moving[1]), moving[2])

    def visit(totals, moving, distance):
        coef_block, valence_block = unpack(moving)
        source = jnp.mod(ka_index + distance, ka_count)
        return accumulate(totals, coef_block, valence_block, source)

    zero_field = jnp.zeros((vector_count, kpoint_count, mu_count, point_count), jnp.float32)
    totals = accumulate((zero_field, zero_field), own_coef, valence, ka_index)
    below_item = payload
    for count_done in range(REACH):
        below_item = advance(below_item, 1)
        totals = visit(totals, below_item, -(count_done + 1))
    above_item = payload
    for count_done in range(REACH):
        above_item = advance(above_item, -1)
        totals = visit(totals, above_item, count_done + 1)
    sum_real = totals[0].astype(jnp.bfloat16)
    sum_imag = totals[1].astype(jnp.bfloat16)
    back_real, back_imag = pair_einsum(
        "bkmn,kvn->bkvm", (sum_real, sum_imag), (valence[0], valence[1]), False
    )
    potential_real = potential[:, 0][:, None, None, :]
    potential_imag = potential[:, 1][:, None, None, :]
    exchange_real = potential_real * valence_part[0] - potential_imag * valence_part[1]
    exchange_imag = potential_real * valence_part[1] + potential_imag * valence_part[0]
    field_real = (exchange_weight * exchange_real - back_real).astype(jnp.bfloat16)
    field_imag = (exchange_weight * exchange_imag - back_imag).astype(jnp.bfloat16)
    out_real, out_imag = pair_einsum(
        "bkvm,kcm->bkvc", (field_real, field_imag), (conduction[0], conduction[1]), True
    )
    partial_out = jnp.stack([out_real, out_imag], axis=1)
    summed = lax.psum_scatter(
        partial_out.astype(jnp.bfloat16), "isdf", scatter_dimension=4, tiled=True
    ).astype(jnp.float32)
    vector_part = lax.dynamic_slice_in_dim(vector, isdf_index * cond_share, cond_share, 4).astype(
        jnp.float32
    )
    channel_out = (energy[None, None] * vector_part + summed).astype(jnp.bfloat16)
    partner_out = swapped(channel_out, "pm", 0)
    blended = (
        0.5 * (partner_out.astype(jnp.float32) + parity * channel_out.astype(jnp.float32))
    ).astype(jnp.bfloat16)
    distant_out = result_bits(blended)
    reflected = conjugated(jnp.take(distant_out, local_mirror, axis=2))
    result = jnp.where(is_plus, blended, reflected)
    return result[None]


def solution(mesh):
    return jax.shard_map(
        per_device,
        mesh=mesh,
        in_specs=(
            P("pm", None, None, "ka", None, None),
            P(None, "ka", None, "isdf"),
            P(None, "ka", None, None),
            P("ka", None, "isdf"),
            P(None, None, "isdf", None),
            P(None, "isdf"),
            P("ka"),
            P("ka", None),
        ),
        out_specs=P("pm", None, None, "ka", None, "isdf"),
        check_vma=False,
    )
```

profile of v0, /device:TPU:2, one launch (start us, length us, event | category | flops | bytes accessed | tf_op | source)
XLA Modules:
  0.0 1090.2 jit_solution(7875653439164302398)
XLA Ops:
  8.6 10.8 collective-permute-start.15
  21.3 5.8 collective-permute-start.16
  28.1 3.5 collective-permute-start
  32.8 3.2 copy.91
  36.0 2.2 fusion.12
  38.2 2.2 fusion.13
  40.6 2.2 fusion.14
  45.2 2.2 fusion.16
  49.8 2.2 fusion.18
  52.0 2.4 fusion.19
  54.6 2.2 fusion.10
  56.8 2.2 fusion.11
  59.0 3.0 fusion.79
  76.7 6.6 collective-permute-done.2
  87.2 12.3 %collective-permute-done.3 = bf16[2,2,2,64,256]{4,3,0,2,1:T(8,128)(2,1)S(1)} collective-permute-done((bf16[2,2,2,64,256]{4,3,0,2,1:T(8,128)(2,1)S(1)}, bf16[2,2,2,64,256]{4,3,0,2,1:T(8,128)(2,1)S(1)}, u32[]{:S(2)}, u32[]{:S(2)}) %collective-permute-start.3) | collective-permute-done | bytes 262176 | tf_op jit(solution)/shard_map/ppermute | solution.py:17
  99.5 2.4 collective-permute-start.4
  104.0 22.7 %collective-permute-done.4 = bf16[2,2,2,64,256]{4,3,0,2,1:T(8,128)(2,1)S(1)} collective-permute-done((bf16[2,2,2,64,256]{4,3,0,2,1:T(8,128)(2,1)S(1)}, bf16[2,2,2,64,256]{4,3,0,2,1:T(8,128)(2,1)S(1)}, u32[]{:S(2)}, u32[]{:S(2)}) %collective-permute-start.4) | collective-permute-done | bytes 262176 | tf_op jit(solution)/shard_map/ppermute | solution.py:17
  126.6 14.7 %collective-permute-start.5 = (bf16[2,2,2,64,256]{4,3,0,2,1:T(8,128)(2,1)S(1)}, bf16[2,2,2,64,256]{4,3,0,2,1:T(8,128)(2,1)S(1)}, u32[]{:S(2)}, u32[]{:S(2)}) collective-permute-start(bf16[2,2,2,64,256]{4,3,0,2,1:T(8,128)(2,1)S(1)} %collective-permute-done.4), channel_id=1, source_target_pairs={{0,32},{32,0},{2,34},{34,2},{4,36},{36,4},{6,38},{38,6},{8,40},{40... | collective-permute-start | bytes 786440 | tf_op jit(solution)/shard_map/ppermute | solution.py:17
  143.4 14.8 %collective-permute-done.5 = bf16[2,2,2,64,256]{4,3,0,2,1:T(8,128)(2,1)S(1)} collective-permute-done((bf16[2,2,2,64,256]{4,3,0,2,1:T(8,128)(2,1)S(1)}, bf16[2,2,2,64,256]{4,3,0,2,1:T(8,128)(2,1)S(1)}, u32[]{:S(2)}, u32[]{:S(2)}) %collective-permute-start.5) | collective-permute-done | bytes 262176 | tf_op jit(solution)/shard_map/ppermute | solution.py:17
  158.2 2.7 collective-permute-start.6
  163.1 5.4 collective-permute-done.6
  168.4 4.2 collective-permute-start.7
  198.8 5.8 collective-permute-start.19
  206.5 5.8 collective-permute-start.18
  214.0 2.2 gather_fusion
  228.5 583.0 %psum.7 = f32[2,2,512]{2,1,0:T(2,128)S(1)} all-reduce(f32[2,2,512]{2,1,0:T(2,128)S(1)} %fusion.90), channel_id=1, replica_groups=mesh['pm'=2,'ka'=128,'isdf'=2] {'ka','isdf'}, use_global_device_ids=true, to_apply=%region_0.1 | all-reduce | flops 2048 | bytes 16384 | tf_op jit(solution)/shard_map/psum | solution.py:99
  828.4 2.2 fusion.76
  830.6 2.7 collective-permute-start.11
  845.6 5.3 collective-permute-start.17
  861.0 2.2 fusion.68
  874.3 2.3 fusion.52
  878.6 9.2 add_convert_fusion
  887.9 9.5 add_convert_fusion.1
  901.8 92.5 %reduce-scatter.4.cloned.1.call-done = bf16[128,512]{1,0:T(8,128)(2,1)} async-done(((bf16[256,512]{1,0:T(8,128)(2,1)}), bf16[128,512]{1,0:T(8,128)(2,1)}) %reduce-scatter.4.cloned.1.call-update) | async-done | bytes 131088
  996.5 2.5 collective-permute-start.20
  999.0 4.7 collective-permute-done.20
  1007.0 3.5 collective-permute-start.22
  1010.4 4.0 collective-permute-done.22
  1014.4 4.4 collective-permute-start.23
  1018.9 5.9 collective-permute-done.23
  1024.7 7.6 collective-permute-start.24
  1032.4 9.9 collective-permute-done.24
  1042.2 12.0 %collective-permute-start.25 = (bf16[2,2,2,64,128]{4,3,0,2,1:T(8,128)(2,1)S(1)}, bf16[2,2,2,64,128]{4,3,0,2,1:T(8,128)(2,1)S(1)}, u32[]{:S(2)}, u32[]{:S(2)}) collective-permute-start(bf16[2,2,2,64,128]{4,3,0,2,1:T(8,128)(2,1)S(1)} %collective-permute-done.24), channel_id=1, source_target_pairs={{0,32},{32,0},{2,34},{34,2},{4,36},{36,4},{6,38},{38,6},{8,40},{40... | collective-permute-start | bytes 393224 | tf_op jit(solution)/shard_map/ppermute | solution.py:17
  1054.2 12.1 %collective-permute-done.25 = bf16[2,2,2,64,128]{4,3,0,2,1:T(8,128)(2,1)S(1)} collective-permute-done((bf16[2,2,2,64,128]{4,3,0,2,1:T(8,128)(2,1)S(1)}, bf16[2,2,2,64,128]{4,3,0,2,1:T(8,128)(2,1)S(1)}, u32[]{:S(2)}, u32[]{:S(2)}) %collective-permute-start.25) | collective-permute-done | bytes 131104 | tf_op jit(solution)/shard_map/ppermute | solution.py:17
  1066.3 2.5 collective-permute-start.26
  1068.8 4.4 collective-permute-done.26
  1073.2 3.9 collective-permute-start.27
  1077.1 4.4 collective-permute-done.27
  (269 shorter events, 140.8 us)
Async XLA Ops:
  6.5 221.4 %copy-start = (f32[512,256]{1,0:T(8,128)S(1)}, f32[512,256]{1,0:T(8,128)}, u32[]{:S(2)}) copy-start(f32[512,256]{1,0:T(8,128)} %param.13) | copy-start | bytes 1572868
  6.5 987.7 %reduce-scatter.4.cloned.1.call-start = ((), (), s32[]{:S(2)}) async-start(), calls=%async_computation.1 | async-start | bytes 393216
  6.5 198.1 %collective-permute-start.9 = (bf16[2,2,256,256]{3,2,1,0:T(8,128)(2,1)}, bf16[2,2,256,256]{3,2,1,0:T(8,128)(2,1)}, u32[]{:S(2)}, u32[]{:S(2)}) collective-permute-start(bf16[2,2,256,256]{3,2,1,0:T(8,128)(2,1)} %param.9), channel_id=1, source_target_pairs={{0,2},{2,4},{4,6},{6,8},{8,10},{10,12},{12,14},{14,16},{16,18},{18... | collective-permute-start | bytes 1572872 | tf_op jit(solution)/shard_map/ppermute | solution.py:22
  8.6 197.9 %collective-permute-start.15 = (bf16[2,2,256,256]{3,2,1,0:T(8,128)(2,1)}, bf16[2,2,256,256]{3,2,1,0:T(8,128)(2,1)}, u32[]{:S(2)}, u32[]{:S(2)}) collective-permute-start(bf16[2,2,256,256]{3,2,1,0:T(8,128)(2,1)} %param.9), channel_id=1, source_target_pairs={{0,254},{2,0},{4,2},{6,4},{8,6},{10,8},{12,10},{14,12},{16,14},{18... | collective-permute-start | bytes 1572872 | tf_op jit(solution)/shard_map/ppermute | solution.py:22
  19.4 177.4 %collective-permute-start.10 = (bf16[2,2,64,512]{3,2,1,0:T(8,128)(2,1)}, bf16[2,2,64,512]{3,2,1,0:T(8,128)(2,1)}, u32[]{:S(2)}, u32[]{:S(2)}) collective-permute-start(bf16[2,2,64,512]{3,2,1,0:T(8,128)(2,1)} %param.10), channel_id=1, source_target_pairs={{0,2},{2,4},{4,6},{6,8},{8,10},{10,12},{12,14},{14,16},{16,18},{18... | collective-permute-start | bytes 786440 | tf_op jit(solution)/shard_map/ppermute | solution.py:22
  21.3 177.5 %collective-permute-start.16 = (bf16[2,2,64,512]{3,2,1,0:T(8,128)(2,1)}, bf16[2,2,64,512]{3,2,1,0:T(8,128)(2,1)}, u32[]{:S(2)}, u32[]{:S(2)}) collective-permute-start(bf16[2,2,64,512]{3,2,1,0:T(8,128)(2,1)} %param.10), channel_id=1, source_target_pairs={{0,254},{2,0},{4,2},{6,4},{8,6},{10,8},{12,10},{14,12},{16,14},{18... | collective-permute-start | bytes 786440 | tf_op jit(solution)/shard_map/ppermute | solution.py:22
  28.1 40.2 %collective-permute-start = (bf16[2,2,2,64,256]{4,3,0,2,1:T(8,128)(2,1)S(1)}, bf16[2,2,2,64,256]{4,3,0,2,1:T(8,128)(2,1)S(1)}, u32[]{:S(2)}, u32[]{:S(2)}) collective-permute-start(bf16[2,2,2,64,256]{4,3,0,2,1:T(8,128)(2,1)S(1)} %bitcast.651), channel_id=1, source_target_pairs={{0,256},{256,0},{1,257},{257,1},{2,258},{258,2},{3,259},{259,3},{4... | collective-permute-start | bytes 786440 | tf_op jit(solution)/shard_map/ppermute | solution.py:17
  68.3 8.4 copy-start.55
  68.3 4.2 collective-permute-start.1
  72.5 12.6 %copy-start.49 = (bf16[2,2,256,512]{3,1,2,0:T(2,128)(2,1)S(1)}, bf16[2,2,256,512]{3,1,2,0:T(2,128)(2,1)}, u32[]{:S(2)}) copy-start(bf16[2,2,256,512]{3,1,2,0:T(2,128)(2,1)} %fusion.18) | copy-start | bytes 3145732
  72.5 10.7 collective-permute-start.2
  76.7 25.3 %copy-start.48 = (bf16[2,2,256,512]{3,1,2,0:T(2,128)(2,1)S(1)}, bf16[2,2,256,512]{3,1,2,0:T(2,128)(2,1)}, u32[]{:S(2)}) copy-start(bf16[2,2,256,512]{3,1,2,0:T(2,128)(2,1)} %fusion.19) | copy-start | bytes 3145732
  83.2 16.3 %collective-permute-start.3 = (bf16[2,2,2,64,256]{4,3,0,2,1:T(8,128)(2,1)S(1)}, bf16[2,2,2,64,256]{4,3,0,2,1:T(8,128)(2,1)S(1)}, u32[]{:S(2)}, u32[]{:S(2)}) collective-permute-start(bf16[2,2,2,64,256]{4,3,0,2,1:T(8,128)(2,1)S(1)} %collective-permute-done.2), channel_id=1, source_target_pairs={{0,8},{8,0},{2,10},{10,2},{4,12},{12,4},{6,14},{14,6},{16,24},{24,... | collective-permute-start | bytes 786440 | tf_op jit(solution)/shard_map/ppermute | solution.py:17
  87.2 54.1 %copy-start.47 = (bf16[2,2,256,512]{3,1,2,0:T(2,128)(2,1)S(1)}, bf16[2,2,256,512]{3,1,2,0:T(2,128)(2,1)}, u32[]{:S(2)}) copy-start(bf16[2,2,256,512]{3,1,2,0:T(2,128)(2,1)} %fusion.10) | copy-start | bytes 3145732
  99.5 27.1 %collective-permute-start.4 = (bf16[2,2,2,64,256]{4,3,0,2,1:T(8,128)(2,1)S(1)}, bf16[2,2,2,64,256]{4,3,0,2,1:T(8,128)(2,1)S(1)}, u32[]{:S(2)}, u32[]{:S(2)}) collective-permute-start(bf16[2,2,2,64,256]{4,3,0,2,1:T(8,128)(2,1)S(1)} %collective-permute-done.3), channel_id=1, source_target_pairs={{0,16},{16,0},{2,18},{18,2},{4,20},{20,4},{6,22},{22,6},{8,24},{24... | collective-permute-start | bytes 786440 | tf_op jit(solution)/shard_map/ppermute | solution.py:17
  103.9 57.0 %copy-start.46 = (bf16[2,2,256,512]{3,1,2,0:T(2,128)(2,1)S(1)}, bf16[2,2,256,512]{3,1,2,0:T(2,128)(2,1)}, u32[]{:S(2)}) copy-start(bf16[2,2,256,512]{3,1,2,0:T(2,128)(2,1)} %fusion.11) | copy-start | bytes 3145732
  126.6 31.6 %collective-permute-start.5 = (bf16[2,2,2,64,256]{4,3,0,2,1:T(8,128)(2,1)S(1)}, bf16[2,2,2,64,256]{4,3,0,2,1:T(8,128)(2,1)S(1)}, u32[]{:S(2)}, u32[]{:S(2)}) collective-permute-start(bf16[2,2,2,64,256]{4,3,0,2,1:T(8,128)(2,1)S(1)} %collective-permute-done.4), channel_id=1, source_target_pairs={{0,32},{32,0},{2,34},{34,2},{4,36},{36,4},{6,38},{38,6},{8,40},{40... | collective-permute-start | bytes 786440 | tf_op jit(solution)/shard_map/ppermute | solution.py:17
  143.4 29.3 %copy-start.59 = (s32[2]{0:T(128)S(1)}, s32[2]{0:T(128)}, u32[]{:S(2)}) copy-start(s32[2]{0:T(128)} %param.14) | copy-start | bytes 28
  158.2 10.2 collective-permute-start.6
  168.4 43.9 %collective-permute-start.7 = (bf16[2,2,2,64,256]{4,3,0,2,1:T(8,128)(2,1)}, bf16[2,2,2,64,256]{4,3,0,2,1:T(8,128)(2,1)}, u32[]{:S(2)}, u32[]{:S(2)}) collective-permute-start(bf16[2,2,2,64,256]{4,3,0,2,1:T(8,128)(2,1)} %collective-permute-done.6), channel_id=1, source_target_pairs={{0,128},{128,0},{2,130},{130,2},{4,132},{132,4},{6,134},{134,6},{8... | collective-permute-start | bytes 786440 | tf_op jit(solution)/shard_map/ppermute | solution.py:17
  196.8 22.3 %copy-start.21 = (bf16[2,2,256,256]{3,2,1,0:T(8,128)(2,1)S(1)}, bf16[2,2,256,256]{3,2,1,0:T(8,128)(2,1)}, u32[]{:S(2)}) copy-start(bf16[2,2,256,256]{3,2,1,0:T(8,128)(2,1)} %param.9) | copy-start | bytes 1572868
  196.8 658.7 %collective-permute-start.13 = (bf16[2,2,64,512]{3,2,1,0:T(8,128)(2,1)}, bf16[2,2,64,512]{3,2,1,0:T(8,128)(2,1)}, u32[]{:S(2)}, u32[]{:S(2)}) collective-permute-start(bf16[2,2,64,512]{3,2,1,0:T(8,128)(2,1)} %collective-permute-done.10), channel_id=1, source_target_pairs={{0,2},{2,4},{4,6},{6,8},{8,10},{10,12},{12,14},{14,16},{16,18},{18... | collective-permute-start | bytes 786440 | tf_op jit(solution)/shard_map/ppermute | solution.py:22
  198.8 669.1 %collective-permute-start.19 = (bf16[2,2,64,512]{3,2,1,0:T(8,128)(2,1)}, bf16[2,2,64,512]{3,2,1,0:T(8,128)(2,1)}, u32[]{:S(2)}, u32[]{:S(2)}) collective-permute-start(bf16[2,2,64,512]{3,2,1,0:T(8,128)(2,1)} %collective-permute-done.16), channel_id=1, source_target_pairs={{0,254},{2,0},{4,2},{6,4},{8,6},{10,8},{12,10},{14,12},{16,14},{18... | collective-permute-start | bytes 786440 | tf_op jit(solution)/shard_map/ppermute | solution.py:22
  204.6 641.0 %collective-permute-start.12 = (bf16[2,2,256,256]{3,2,1,0:T(8,128)(2,1)}, bf16[2,2,256,256]{3,2,1,0:T(8,128)(2,1)}, u32[]{:S(2)}, u32[]{:S(2)}) collective-permute-start(bf16[2,2,256,256]{3,2,1,0:T(8,128)(2,1)} %collective-permute-done.9), channel_id=1, source_target_pairs={{0,2},{2,4},{4,6},{6,8},{8,10},{10,12},{12,14},{14,16},{16,18},{18... | collective-permute-start | bytes 1572872 | tf_op jit(solution)/shard_map/ppermute | solution.py:22
  206.5 656.7 %collective-permute-start.18 = (bf16[2,2,256,256]{3,2,1,0:T(8,128)(2,1)}, bf16[2,2,256,256]{3,2,1,0:T(8,128)(2,1)}, u32[]{:S(2)}, u32[]{:S(2)}) collective-permute-start(bf16[2,2,256,256]{3,2,1,0:T(8,128)(2,1)} %collective-permute-done.15), channel_id=1, source_target_pairs={{0,254},{2,0},{4,2},{6,4},{8,6},{10,8},{12,10},{14,12},{16,14},{18... | collective-permute-start | bytes 1572872 | tf_op jit(solution)/shard_map/ppermute | solution.py:22
  219.1 7.1 copy-start.57
  221.3 594.7 %collective-permute-start.8 = (bf16[2,2,2,64,256]{4,3,0,2,1:T(8,128)(2,1)}, bf16[2,2,2,64,256]{4,3,0,2,1:T(8,128)(2,1)}, u32[]{:S(2)}, u32[]{:S(2)}) collective-permute-start(bf16[2,2,2,64,256]{4,3,0,2,1:T(8,128)(2,1)} %fusion.89), channel_id=1, source_target_pairs={{0,2},{2,4},{4,6},{6,8},{8,10},{10,12},{12,14},{14,16},{16,18},{18... | collective-permute-start | bytes 786440 | tf_op jit(solution)/shard_map/ppermute | solution.py:22
  228.5 584.7 %copy-start.45 = (bf16[2,2,64,256]{3,2,1,0:T(8,128)(2,1)S(1)}, bf16[2,2,64,256]{3,2,1,0:T(8,128)(2,1)}, u32[]{:S(2)}) copy-start(bf16[2,2,64,256]{3,2,1,0:T(8,128)(2,1)} %get-tuple-element.66) | copy-start | bytes 393220
  816.0 60.6 %copy-start.20 = (f32[2,256,512]{2,1,0:T(8,128)}, f32[2,256,512]{2,1,0:T(8,128)S(1)}, u32[]{:S(2)}) copy-start(f32[2,256,512]{2,1,0:T(8,128)S(1)} %get-tuple-element.15) | copy-start | bytes 3145732
  816.0 14.6 %collective-permute-start.14 = (bf16[2,2,2,64,256]{4,3,0,2,1:T(8,128)(2,1)}, bf16[2,2,2,64,256]{4,3,0,2,1:T(8,128)(2,1)S(1)}, u32[]{:S(2)}, u32[]{:S(2)}) collective-permute-start(bf16[2,2,2,64,256]{4,3,0,2,1:T(8,128)(2,1)} %fusion.89), channel_id=1, source_target_pairs={{0,254},{2,0},{4,2},{6,4},{8,6},{10,8},{12,10},{14,12},{16,14},{18... | collective-permute-start | bytes 786440 | tf_op jit(solution)/shard_map/ppermute | solution.py:22
  830.6 20.3 %collective-permute-start.11 = (bf16[2,2,2,64,256]{4,3,0,2,1:T(8,128)(2,1)}, bf16[2,2,2,64,256]{4,3,0,2,1:T(8,128)(2,1)S(1)}, u32[]{:S(2)}, u32[]{:S(2)}) collective-permute-start(bf16[2,2,2,64,256]{4,3,0,2,1:T(8,128)(2,1)} %collective-permute-done.8), channel_id=1, source_target_pairs={{0,2},{2,4},{4,6},{6,8},{8,10},{10,12},{12,14},{14,16},{16,18},{18... | collective-permute-start | bytes 786440 | tf_op jit(solution)/shard_map/ppermute | solution.py:22
  845.6 17.6 %collective-permute-start.17 = (bf16[2,2,2,64,256]{4,3,0,2,1:T(8,128)(2,1)S(1)}, bf16[2,2,2,64,256]{4,3,0,2,1:T(8,128)(2,1)S(1)}, u32[]{:S(2)}, u32[]{:S(2)}) collective-permute-start(bf16[2,2,2,64,256]{4,3,0,2,1:T(8,128)(2,1)S(1)} %collective-permute-done.14), channel_id=1, source_target_pairs={{0,254},{2,0},{4,2},{6,4},{8,6},{10,8},{12,10},{14,12},{16,14},{18... | collective-permute-start | bytes 786440 | tf_op jit(solution)/shard_map/ppermute | solution.py:22
  865.5 11.0 %copy-start.19 = (f32[2,256,512]{2,1,0:T(8,128)S(1)}, f32[2,256,512]{2,1,0:T(8,128)}, u32[]{:S(2)}) copy-start(f32[2,256,512]{2,1,0:T(8,128)} %copy.99) | copy-start | bytes 3145732
  867.9 8.6 copy-start.16
  868.0 8.6 copy-start.17
  868.0 8.6 copy-start.18
  869.5 7.1 copy-start.14
  869.5 7.1 copy-start.15
  900.0 95.6 %copy-start.58 = (f32[2,64,128]{2,1,0:T(8,128)S(1)}, f32[2,64,128]{2,1,0:T(8,128)}, u32[]{:S(2)}) copy-start(f32[2,64,128]{2,1,0:T(8,128)} %param.11) | copy-start | bytes 196612
  900.7 182.2 %copy-start.1 = (f32[512,256]{1,0:T(8,128)S(1)}, f32[512,256]{1,0:T(8,128)}, u32[]{:S(2)}) copy-start(f32[512,256]{1,0:T(8,128)} %param.13) | copy-start | bytes 1572868
  996.5 7.1 collective-permute-start.20
  1003.7 3.2 collective-permute-start.21
  1007.0 7.4 collective-permute-start.22
  1014.4 10.3 collective-permute-start.23
  1024.7 17.5 %collective-permute-start.24 = (bf16[2,2,2,64,128]{4,3,0,2,1:T(8,128)(2,1)S(1)}, bf16[2,2,2,64,128]{4,3,0,2,1:T(8,128)(2,1)S(1)}, u32[]{:S(2)}, u32[]{:S(2)}) collective-permute-start(bf16[2,2,2,64,128]{4,3,0,2,1:T(8,128)(2,1)S(1)} %collective-permute-done.23), channel_id=1, source_target_pairs={{0,16},{16,0},{2,18},{18,2},{4,20},{20,4},{6,22},{22,6},{8,24},{24... | collective-permute-start | bytes 393224 | tf_op jit(solution)/shard_map/ppermute | solution.py:17
  1042.2 24.1 %collective-permute-start.25 = (bf16[2,2,2,64,128]{4,3,0,2,1:T(8,128)(2,1)S(1)}, bf16[2,2,2,64,128]{4,3,0,2,1:T(8,128)(2,1)S(1)}, u32[]{:S(2)}, u32[]{:S(2)}) collective-permute-start(bf16[2,2,2,64,128]{4,3,0,2,1:T(8,128)(2,1)S(1)} %collective-permute-done.24), channel_id=1, source_target_pairs={{0,32},{32,0},{2,34},{34,2},{4,36},{36,4},{6,38},{38,6},{8,40},{40... | collective-permute-start | bytes 393224 | tf_op jit(solution)/shard_map/ppermute | solution.py:17
  1066.3 6.8 collective-permute-start.26
  1073.2 8.4 collective-permute-start.27
  (41 other events, 124.6 us)
Sparse Core Ops, SparseCore 0:
  901.9 92.3 reduce-scatter.3
where the time goes:
time: 1100 us; the launch traced here: 1090 us
  blocking collectives  583 us (53%)
  waiting for transfers between devices  201 us (18%)
  starting transfers between devices  120 us (11%)
  matrix products  76.2 us (7%)
  other arithmetic  56.5 us (5%)
  local copies, waits for them, and re-layouts  38.9 us (4%)
  between operations  15.1 us (1%)
    psum x1, blocking collectives, per_device(): spread = lax.psum(spread, ('ka', 'isdf'))  583 us
    ppermute x16, waiting for transfers between devices, swapped(): return lax.ppermute(block, axis, route)  108 us
    unnamed x2, waiting for transfers between devices  92.5 us
    ppermute x16, starting transfers between devices, swapped(): return lax.ppermute(block, axis, route)  71.8 us
    dot_general x48, matrix products, single(): jnp.einsum(pattern, first, second, preferred_element_type=jnp.float32)  53.3 us
    ppermute x12, starting transfers between devices, shifted(): lax.ppermute(value, axis, [(i, (i + by) % size) for i in range(size)])  47.7 us
    dot_general x10, matrix products, accumulate(): jnp.einsum('kw,wrmn->rkmn', selector[:, visitor], screened, preferred_ele...  22.4 us
  transfers between devices with their start and end apart: 29, of which 14 were waited for; matrix products, arithmetic and copies ran while one was open for 12% of the time, Pallas kernels for 0%

commit v1 on v0

--- a/solution.py
+++ b/solution.py
@@ -96,7 +96,10 @@
     )
     density = jnp.stack([rho_real, rho_imag], axis=1)
     spread = jnp.einsum("nm,brm->brn", coulomb, density, precision=HIGHEST)
-    spread = lax.psum(spread, ("ka", "isdf"))
+    xx = spread
+    for ii in ("ka", "isdf"):
+        xx = jax.lax.psum(xx, ii)
+    spread = xx
     potential = lax.dynamic_slice_in_dim(spread, isdf_index * mu_count, mu_count, 2)
     class_ids = jnp.arange(screened.shape[0], dtype=jnp.int32)
 

time: 1100 us -> 704 us (0.64)
  the two profiles are of different devices: /device:TPU:2 before, /device:TPU:6 now
where the time goes in v1:
time: 704 us; the launch traced here: 694 us
  blocking collectives  223 us (32%)
  waiting for transfers between devices  166 us (24%)
  starting transfers between devices  118 us (17%)
  matrix products  76.2 us (11%)
  other arithmetic  56.4 us (8%)
  local copies, waits for them, and re-layouts  38.9 us (6%)
  between operations  15.1 us (2%)
    psum x2, blocking collectives, per_device(): xx = jax.lax.psum(xx, ii)  223 us
    ppermute x16, waiting for transfers between devices, swapped(): return lax.ppermute(block, axis, route)  109 us
    ppermute x16, starting transfers between devices, swapped(): return lax.ppermute(block, axis, route)  70.1 us
    unnamed x2, waiting for transfers between devices  57.2 us
    dot_general x48, matrix products, single(): jnp.einsum(pattern, first, second, preferred_element_type=jnp.float32)  53.3 us
    ppermute x12, starting transfers between devices, shifted(): lax.ppermute(value, axis, [(i, (i + by) % size) for i in range(size)])  48 us
    dot_general x10, matrix products, accumulate(): jnp.einsum('kw,wrmn->rkmn', selector[:, visitor], screened, preferred_ele...  22.3 us
    mul x10, other arithmetic, accumulate(): screen_real * visit_real - screen_imag * visit_imag  21.6 us
  transfers between devices with their start and end apart: 29, of which 14 were waited for; matrix products, arithmetic and copies ran while one was open for 19% of the time, Pallas kernels for 0%

profile of v1, /device:TPU:6, one launch (start us, length us, event | category | flops | bytes accessed | tf_op | source)
XLA Modules:
  0.0 693.6 jit_solution(5122850828781368609)
XLA Ops:
  8.6 11.1 %collective-permute-start.15 = (bf16[2,2,256,256]{3,2,1,0:T(8,128)(2,1)}, bf16[2,2,256,256]{3,2,1,0:T(8,128)(2,1)}, u32[]{:S(2)}, u32[]{:S(2)}) collective-permute-start(bf16[2,2,256,256]{3,2,1,0:T(8,128)(2,1)} %param.9), channel_id=1, source_target_pairs={{0,254},{2,0},{4,2},{6,4},{8,6},{10,8},{12,10},{14,12},{16,14},{18... | collective-permute-start | bytes 1572872 | tf_op jit(solution)/shard_map/ppermute | solution.py:22
  21.6 5.8 collective-permute-start.16
  28.4 3.5 collective-permute-start
  33.1 3.2 copy.91
  36.3 2.2 fusion.12
  40.9 2.2 fusion.14
  45.5 2.2 fusion.16
  50.1 2.2 fusion.18
  52.3 2.4 fusion.19
  54.9 2.2 fusion.10
  57.1 2.2 fusion.11
  59.3 3.0 fusion.79
  76.9 6.6 collective-permute-done.2
  87.4 12.3 %collective-permute-done.3 = bf16[2,2,2,64,256]{4,3,0,2,1:T(8,128)(2,1)S(1)} collective-permute-done((bf16[2,2,2,64,256]{4,3,0,2,1:T(8,128)(2,1)S(1)}, bf16[2,2,2,64,256]{4,3,0,2,1:T(8,128)(2,1)S(1)}, u32[]{:S(2)}, u32[]{:S(2)}) %collective-permute-start.3) | collective-permute-done | bytes 262176 | tf_op jit(solution)/shard_map/ppermute | solution.py:17
  103.9 23.0 %collective-permute-done.4 = bf16[2,2,2,64,256]{4,3,0,2,1:T(8,128)(2,1)S(1)} collective-permute-done((bf16[2,2,2,64,256]{4,3,0,2,1:T(8,128)(2,1)S(1)}, bf16[2,2,2,64,256]{4,3,0,2,1:T(8,128)(2,1)S(1)}, u32[]{:S(2)}, u32[]{:S(2)}) %collective-permute-start.4) | collective-permute-done | bytes 262176 | tf_op jit(solution)/shard_map/ppermute | solution.py:17
  126.9 14.4 %collective-permute-start.5 = (bf16[2,2,2,64,256]{4,3,0,2,1:T(8,128)(2,1)S(1)}, bf16[2,2,2,64,256]{4,3,0,2,1:T(8,128)(2,1)S(1)}, u32[]{:S(2)}, u32[]{:S(2)}) collective-permute-start(bf16[2,2,2,64,256]{4,3,0,2,1:T(8,128)(2,1)S(1)} %collective-permute-done.4), channel_id=1, source_target_pairs={{0,32},{32,0},{2,34},{34,2},{4,36},{36,4},{6,38},{38,6},{8,40},{40... | collective-permute-start | bytes 786440 | tf_op jit(solution)/shard_map/ppermute | solution.py:17
  143.3 14.9 %collective-permute-done.5 = bf16[2,2,2,64,256]{4,3,0,2,1:T(8,128)(2,1)S(1)} collective-permute-done((bf16[2,2,2,64,256]{4,3,0,2,1:T(8,128)(2,1)S(1)}, bf16[2,2,2,64,256]{4,3,0,2,1:T(8,128)(2,1)S(1)}, u32[]{:S(2)}, u32[]{:S(2)}) %collective-permute-start.5) | collective-permute-done | bytes 262176 | tf_op jit(solution)/shard_map/ppermute | solution.py:17
  158.2 2.7 collective-permute-start.6
  163.1 5.3 collective-permute-done.6
  168.4 3.5 collective-permute-start.7
  198.0 5.8 collective-permute-start.19
  205.7 5.8 collective-permute-start.18
  213.2 2.2 gather_fusion
  227.7 216.0 %psum.14 = f32[2,2,512]{2,1,0:T(2,128)S(1)} all-reduce(f32[2,2,512]{2,1,0:T(2,128)S(1)} %fusion.90), channel_id=1, replica_groups=mesh['pm'=2,'ka'=128,'isdf'=2] {'ka'}, use_global_device_ids=true, to_apply=%region_0.1 | all-reduce | flops 2048 | bytes 16384 | tf_op jit(solution)/shard_map/psum | solution.py:101
  443.7 6.5 psum.15
  467.1 2.2 fusion.76
  469.3 2.7 collective-permute-start.11
  482.1 2.2 fusion.60
  484.3 5.3 collective-permute-start.17
  499.7 2.2 fusion.68
  513.0 2.3 fusion.52
  517.3 9.2 %add_convert_fusion = bf16[2,2,256,512]{3,2,0,1:T(8,128)(2,1)S(1)} fusion(f32[2,256,512]{2,1,0:T(8,128)} %get-tuple-element.48, f32[2,256,512]{2,1,0:T(8,128)S(1)} %copy-done.14, f32[2,256,512]{2,1,0:T(8,128)} %get-tuple-element.69, f32[2,256,512]{2,1,0:T(8,128)S(1)} %copy-done.13, f32[2,256,512]{2,1,0:T(8,128)} %get-tuple-element.47, ...), kind=kLoop, calls=%fused_computation.2 | loop fusion | flops 20971520 | bytes 42991616 | tf_op jit(solution)/shard_map/convert_element_type | solution.py:154
  526.6 9.5 %add_convert_fusion.1 = bf16[2,2,256,512]{3,2,0,1:T(8,128)(2,1)S(1)} fusion(f32[2,256,512]{2,1,0:T(8,128)} %get-tuple-element.48, f32[2,256,512]{2,1,0:T(8,128)S(1)} %copy-done.14, f32[2,256,512]{2,1,0:T(8,128)} %get-tuple-element.69, f32[2,256,512]{2,1,0:T(8,128)S(1)} %copy-done.13, f32[2,256,512]{2,1,0:T(8,128)} %get-tuple-element.47, ...), kind=kLoop, calls=%fused_computation.3 | loop fusion | flops 20971520 | bytes 42991616 | tf_op jit(solution)/shard_map/convert_element_type | solution.py:153
  540.4 57.2 %reduce-scatter.4.cloned.1.call-done = bf16[128,512]{1,0:T(8,128)(2,1)} async-done(((bf16[256,512]{1,0:T(8,128)(2,1)}), bf16[128,512]{1,0:T(8,128)(2,1)}) %reduce-scatter.4.cloned.1.call-update) | async-done | bytes 131088
  599.9 2.5 collective-permute-start.20
  602.4 4.6 collective-permute-done.20
  610.3 3.5 collective-permute-start.22
  613.8 4.0 collective-permute-done.22
  617.7 4.5 collective-permute-start.23
  622.2 5.8 collective-permute-done.23
  628.1 7.6 %collective-permute-start.24 = (bf16[2,2,2,64,128]{4,3,0,2,1:T(8,128)(2,1)S(1)}, bf16[2,2,2,64,128]{4,3,0,2,1:T(8,128)(2,1)S(1)}, u32[]{:S(2)}, u32[]{:S(2)}) collective-permute-start(bf16[2,2,2,64,128]{4,3,0,2,1:T(8,128)(2,1)S(1)} %collective-permute-done.23), channel_id=1, source_target_pairs={{0,16},{16,0},{2,18},{18,2},{4,20},{20,4},{6,22},{22,6},{8,24},{24... | collective-permute-start | bytes 393224 | tf_op jit(solution)/shard_map/ppermute | solution.py:17
  635.7 9.9 %collective-permute-done.24 = bf16[2,2,2,64,128]{4,3,0,2,1:T(8,128)(2,1)S(1)} collective-permute-done((bf16[2,2,2,64,128]{4,3,0,2,1:T(8,128)(2,1)S(1)}, bf16[2,2,2,64,128]{4,3,0,2,1:T(8,128)(2,1)S(1)}, u32[]{:S(2)}, u32[]{:S(2)}) %collective-permute-start.24) | collective-permute-done | bytes 131104 | tf_op jit(solution)/shard_map/ppermute | solution.py:17
  645.6 12.0 %collective-permute-start.25 = (bf16[2,2,2,64,128]{4,3,0,2,1:T(8,128)(2,1)S(1)}, bf16[2,2,2,64,128]{4,3,0,2,1:T(8,128)(2,1)S(1)}, u32[]{:S(2)}, u32[]{:S(2)}) collective-permute-start(bf16[2,2,2,64,128]{4,3,0,2,1:T(8,128)(2,1)S(1)} %collective-permute-done.24), channel_id=1, source_target_pairs={{0,32},{32,0},{2,34},{34,2},{4,36},{36,4},{6,38},{38,6},{8,40},{40... | collective-permute-start | bytes 393224 | tf_op jit(solution)/shard_map/ppermute | solution.py:17
  657.6 12.1 %collective-permute-done.25 = bf16[2,2,2,64,128]{4,3,0,2,1:T(8,128)(2,1)S(1)} collective-permute-done((bf16[2,2,2,64,128]{4,3,0,2,1:T(8,128)(2,1)S(1)}, bf16[2,2,2,64,128]{4,3,0,2,1:T(8,128)(2,1)S(1)}, u32[]{:S(2)}, u32[]{:S(2)}) %collective-permute-start.25) | collective-permute-done | bytes 131104 | tf_op jit(solution)/shard_map/ppermute | solution.py:17
  669.7 2.6 collective-permute-start.26
  672.3 4.2 collective-permute-done.26
  676.5 3.2 collective-permute-start.27
  679.8 5.1 collective-permute-done.27
  (270 shorter events, 142.8 us)
Async XLA Ops:
  6.5 220.6 %copy-start = (f32[512,256]{1,0:T(8,128)S(1)}, f32[512,256]{1,0:T(8,128)}, u32[]{:S(2)}) copy-start(f32[512,256]{1,0:T(8,128)} %param.13) | copy-start | bytes 1572868
  6.5 591.1 %reduce-scatter.4.cloned.1.call-start = ((), (), s32[]{:S(2)}) async-start(), calls=%async_computation.1 | async-start | bytes 393216
  6.5 197.3 %collective-permute-start.9 = (bf16[2,2,256,256]{3,2,1,0:T(8,128)(2,1)}, bf16[2,2,256,256]{3,2,1,0:T(8,128)(2,1)}, u32[]{:S(2)}, u32[]{:S(2)}) collective-permute-start(bf16[2,2,256,256]{3,2,1,0:T(8,128)(2,1)} %param.9), channel_id=1, source_target_pairs={{0,2},{2,4},{4,6},{6,8},{8,10},{10,12},{12,14},{14,16},{16,18},{18... | collective-permute-start | bytes 1572872 | tf_op jit(solution)/shard_map/ppermute | solution.py:22
  8.6 197.1 %collective-permute-start.15 = (bf16[2,2,256,256]{3,2,1,0:T(8,128)(2,1)}, bf16[2,2,256,256]{3,2,1,0:T(8,128)(2,1)}, u32[]{:S(2)}, u32[]{:S(2)}) collective-permute-start(bf16[2,2,256,256]{3,2,1,0:T(8,128)(2,1)} %param.9), channel_id=1, source_target_pairs={{0,254},{2,0},{4,2},{6,4},{8,6},{10,8},{12,10},{14,12},{16,14},{18... | collective-permute-start | bytes 1572872 | tf_op jit(solution)/shard_map/ppermute | solution.py:22
  19.7 176.3 %collective-permute-start.10 = (bf16[2,2,64,512]{3,2,1,0:T(8,128)(2,1)}, bf16[2,2,64,512]{3,2,1,0:T(8,128)(2,1)}, u32[]{:S(2)}, u32[]{:S(2)}) collective-permute-start(bf16[2,2,64,512]{3,2,1,0:T(8,128)(2,1)} %param.10), channel_id=1, source_target_pairs={{0,2},{2,4},{4,6},{6,8},{8,10},{10,12},{12,14},{14,16},{16,18},{18... | collective-permute-start | bytes 786440 | tf_op jit(solution)/shard_map/ppermute | solution.py:22
  21.6 176.4 %collective-permute-start.16 = (bf16[2,2,64,512]{3,2,1,0:T(8,128)(2,1)}, bf16[2,2,64,512]{3,2,1,0:T(8,128)(2,1)}, u32[]{:S(2)}, u32[]{:S(2)}) collective-permute-start(bf16[2,2,64,512]{3,2,1,0:T(8,128)(2,1)} %param.10), channel_id=1, source_target_pairs={{0,254},{2,0},{4,2},{6,4},{8,6},{10,8},{12,10},{14,12},{16,14},{18... | collective-permute-start | bytes 786440 | tf_op jit(solution)/shard_map/ppermute | solution.py:22
  28.4 40.2 %collective-permute-start = (bf16[2,2,2,64,256]{4,3,0,2,1:T(8,128)(2,1)S(1)}, bf16[2,2,2,64,256]{4,3,0,2,1:T(8,128)(2,1)S(1)}, u32[]{:S(2)}, u32[]{:S(2)}) collective-permute-start(bf16[2,2,2,64,256]{4,3,0,2,1:T(8,128)(2,1)S(1)} %bitcast.651), channel_id=1, source_target_pairs={{0,256},{256,0},{1,257},{257,1},{2,258},{258,2},{3,259},{259,3},{4... | collective-permute-start | bytes 786440 | tf_op jit(solution)/shard_map/ppermute | solution.py:17
  68.6 8.3 %copy-start.55 = (bf16[2,2,2,64,256]{4,3,0,2,1:T(8,128)(2,1)}, bf16[2,2,2,64,256]{4,3,0,2,1:T(8,128)(2,1)S(1)}, u32[]{:S(2)}) copy-start(bf16[2,2,2,64,256]{4,3,0,2,1:T(8,128)(2,1)S(1)} %collective-permute-done) | copy-start | bytes 786436
  68.6 4.2 collective-permute-start.1
  72.8 12.6 %copy-start.49 = (bf16[2,2,256,512]{3,1,2,0:T(2,128)(2,1)S(1)}, bf16[2,2,256,512]{3,1,2,0:T(2,128)(2,1)}, u32[]{:S(2)}) copy-start(bf16[2,2,256,512]{3,1,2,0:T(2,128)(2,1)} %fusion.18) | copy-start | bytes 3145732
  72.8 10.7 %collective-permute-start.2 = (bf16[2,2,2,64,256]{4,3,0,2,1:T(8,128)(2,1)S(1)}, bf16[2,2,2,64,256]{4,3,0,2,1:T(8,128)(2,1)S(1)}, u32[]{:S(2)}, u32[]{:S(2)}) collective-permute-start(bf16[2,2,2,64,256]{4,3,0,2,1:T(8,128)(2,1)S(1)} %collective-permute-done.1), channel_id=1, source_target_pairs={{0,4},{4,0},{2,6},{6,2},{8,12},{12,8},{10,14},{14,10},{16,20},{20,... | collective-permute-start | bytes 786440 | tf_op jit(solution)/shard_map/ppermute | solution.py:17
  76.9 25.0 %copy-start.48 = (bf16[2,2,256,512]{3,1,2,0:T(2,128)(2,1)S(1)}, bf16[2,2,256,512]{3,1,2,0:T(2,128)(2,1)}, u32[]{:S(2)}) copy-start(bf16[2,2,256,512]{3,1,2,0:T(2,128)(2,1)} %fusion.19) | copy-start | bytes 3145732
  83.5 16.3 %collective-permute-start.3 = (bf16[2,2,2,64,256]{4,3,0,2,1:T(8,128)(2,1)S(1)}, bf16[2,2,2,64,256]{4,3,0,2,1:T(8,128)(2,1)S(1)}, u32[]{:S(2)}, u32[]{:S(2)}) collective-permute-start(bf16[2,2,2,64,256]{4,3,0,2,1:T(8,128)(2,1)S(1)} %collective-permute-done.2), channel_id=1, source_target_pairs={{0,8},{8,0},{2,10},{10,2},{4,12},{12,4},{6,14},{14,6},{16,24},{24,... | collective-permute-start | bytes 786440 | tf_op jit(solution)/shard_map/ppermute | solution.py:17
  87.4 53.8 %copy-start.47 = (bf16[2,2,256,512]{3,1,2,0:T(2,128)(2,1)S(1)}, bf16[2,2,256,512]{3,1,2,0:T(2,128)(2,1)}, u32[]{:S(2)}) copy-start(bf16[2,2,256,512]{3,1,2,0:T(2,128)(2,1)} %fusion.10) | copy-start | bytes 3145732
  99.8 27.1 %collective-permute-start.4 = (bf16[2,2,2,64,256]{4,3,0,2,1:T(8,128)(2,1)S(1)}, bf16[2,2,2,64,256]{4,3,0,2,1:T(8,128)(2,1)S(1)}, u32[]{:S(2)}, u32[]{:S(2)}) collective-permute-start(bf16[2,2,2,64,256]{4,3,0,2,1:T(8,128)(2,1)S(1)} %collective-permute-done.3), channel_id=1, source_target_pairs={{0,16},{16,0},{2,18},{18,2},{4,20},{20,4},{6,22},{22,6},{8,24},{24... | collective-permute-start | bytes 786440 | tf_op jit(solution)/shard_map/ppermute | solution.py:17
  103.9 57.0 %copy-start.46 = (bf16[2,2,256,512]{3,1,2,0:T(2,128)(2,1)S(1)}, bf16[2,2,256,512]{3,1,2,0:T(2,128)(2,1)}, u32[]{:S(2)}) copy-start(bf16[2,2,256,512]{3,1,2,0:T(2,128)(2,1)} %fusion.11) | copy-start | bytes 3145732
  126.9 31.3 %collective-permute-start.5 = (bf16[2,2,2,64,256]{4,3,0,2,1:T(8,128)(2,1)S(1)}, bf16[2,2,2,64,256]{4,3,0,2,1:T(8,128)(2,1)S(1)}, u32[]{:S(2)}, u32[]{:S(2)}) collective-permute-start(bf16[2,2,2,64,256]{4,3,0,2,1:T(8,128)(2,1)S(1)} %collective-permute-done.4), channel_id=1, source_target_pairs={{0,32},{32,0},{2,34},{34,2},{4,36},{36,4},{6,38},{38,6},{8,40},{40... | collective-permute-start | bytes 786440 | tf_op jit(solution)/shard_map/ppermute | solution.py:17
  143.3 28.6 %copy-start.59 = (s32[2]{0:T(128)S(1)}, s32[2]{0:T(128)}, u32[]{:S(2)}) copy-start(s32[2]{0:T(128)} %param.14) | copy-start | bytes 28
  158.2 10.2 %collective-permute-start.6 = (bf16[2,2,2,64,256]{4,3,0,2,1:T(8,128)(2,1)S(1)}, bf16[2,2,2,64,256]{4,3,0,2,1:T(8,128)(2,1)}, u32[]{:S(2)}, u32[]{:S(2)}) collective-permute-start(bf16[2,2,2,64,256]{4,3,0,2,1:T(8,128)(2,1)S(1)} %collective-permute-done.5), channel_id=1, source_target_pairs={{0,64},{64,0},{2,66},{66,2},{4,68},{68,4},{6,70},{70,6},{8,72},{72... | collective-permute-start | bytes 786440 | tf_op jit(solution)/shard_map/ppermute | solution.py:17
  168.4 43.1 %collective-permute-start.7 = (bf16[2,2,2,64,256]{4,3,0,2,1:T(8,128)(2,1)}, bf16[2,2,2,64,256]{4,3,0,2,1:T(8,128)(2,1)}, u32[]{:S(2)}, u32[]{:S(2)}) collective-permute-start(bf16[2,2,2,64,256]{4,3,0,2,1:T(8,128)(2,1)} %collective-permute-done.6), channel_id=1, source_target_pairs={{0,128},{128,0},{2,130},{130,2},{4,132},{132,4},{6,134},{134,6},{8... | collective-permute-start | bytes 786440 | tf_op jit(solution)/shard_map/ppermute | solution.py:17
  196.0 22.3 %copy-start.21 = (bf16[2,2,256,256]{3,2,1,0:T(8,128)(2,1)S(1)}, bf16[2,2,256,256]{3,2,1,0:T(8,128)(2,1)}, u32[]{:S(2)}) copy-start(bf16[2,2,256,256]{3,2,1,0:T(8,128)(2,1)} %param.9) | copy-start | bytes 1572868
  196.0 298.2 %collective-permute-start.13 = (bf16[2,2,64,512]{3,2,1,0:T(8,128)(2,1)}, bf16[2,2,64,512]{3,2,1,0:T(8,128)(2,1)}, u32[]{:S(2)}, u32[]{:S(2)}) collective-permute-start(bf16[2,2,64,512]{3,2,1,0:T(8,128)(2,1)} %collective-permute-done.10), channel_id=1, source_target_pairs={{0,2},{2,4},{4,6},{6,8},{8,10},{10,12},{12,14},{14,16},{16,18},{18... | collective-permute-start | bytes 786440 | tf_op jit(solution)/shard_map/ppermute | solution.py:22
  198.0 308.6 %collective-permute-start.19 = (bf16[2,2,64,512]{3,2,1,0:T(8,128)(2,1)}, bf16[2,2,64,512]{3,2,1,0:T(8,128)(2,1)}, u32[]{:S(2)}, u32[]{:S(2)}) collective-permute-start(bf16[2,2,64,512]{3,2,1,0:T(8,128)(2,1)} %collective-permute-done.16), channel_id=1, source_target_pairs={{0,254},{2,0},{4,2},{6,4},{8,6},{10,8},{12,10},{14,12},{16,14},{18... | collective-permute-start | bytes 786440 | tf_op jit(solution)/shard_map/ppermute | solution.py:22
  203.8 280.5 %collective-permute-start.12 = (bf16[2,2,256,256]{3,2,1,0:T(8,128)(2,1)}, bf16[2,2,256,256]{3,2,1,0:T(8,128)(2,1)}, u32[]{:S(2)}, u32[]{:S(2)}) collective-permute-start(bf16[2,2,256,256]{3,2,1,0:T(8,128)(2,1)} %collective-permute-done.9), channel_id=1, source_target_pairs={{0,2},{2,4},{4,6},{6,8},{8,10},{10,12},{12,14},{14,16},{16,18},{18... | collective-permute-start | bytes 1572872 | tf_op jit(solution)/shard_map/ppermute | solution.py:22
  205.7 296.2 %collective-permute-start.18 = (bf16[2,2,256,256]{3,2,1,0:T(8,128)(2,1)}, bf16[2,2,256,256]{3,2,1,0:T(8,128)(2,1)}, u32[]{:S(2)}, u32[]{:S(2)}) collective-permute-start(bf16[2,2,256,256]{3,2,1,0:T(8,128)(2,1)} %collective-permute-done.15), channel_id=1, source_target_pairs={{0,254},{2,0},{4,2},{6,4},{8,6},{10,8},{12,10},{14,12},{16,14},{18... | collective-permute-start | bytes 1572872 | tf_op jit(solution)/shard_map/ppermute | solution.py:22
  218.3 7.1 %copy-start.57 = (f32[256,2,64]{0,2,1:T(8,128)S(1)}, f32[256,2,64]{0,2,1:T(8,128)}, u32[]{:S(2)}) copy-start(f32[256,2,64]{0,2,1:T(8,128)} %get-tuple-element.55) | copy-start | bytes 393220
  220.5 234.2 %collective-permute-start.8 = (bf16[2,2,2,64,256]{4,3,0,2,1:T(8,128)(2,1)}, bf16[2,2,2,64,256]{4,3,0,2,1:T(8,128)(2,1)}, u32[]{:S(2)}, u32[]{:S(2)}) collective-permute-start(bf16[2,2,2,64,256]{4,3,0,2,1:T(8,128)(2,1)} %fusion.89), channel_id=1, source_target_pairs={{0,2},{2,4},{4,6},{6,8},{8,10},{10,12},{12,14},{14,16},{16,18},{18... | collective-permute-start | bytes 786440 | tf_op jit(solution)/shard_map/ppermute | solution.py:22
  227.7 224.2 %copy-start.45 = (bf16[2,2,64,256]{3,2,1,0:T(8,128)(2,1)S(1)}, bf16[2,2,64,256]{3,2,1,0:T(8,128)(2,1)}, u32[]{:S(2)}) copy-start(bf16[2,2,64,256]{3,2,1,0:T(8,128)(2,1)} %get-tuple-element.66) | copy-start | bytes 393220
  454.7 60.6 %copy-start.20 = (f32[2,256,512]{2,1,0:T(8,128)}, f32[2,256,512]{2,1,0:T(8,128)S(1)}, u32[]{:S(2)}) copy-start(f32[2,256,512]{2,1,0:T(8,128)S(1)} %get-tuple-element.15) | copy-start | bytes 3145732
  454.7 14.6 %collective-permute-start.14 = (bf16[2,2,2,64,256]{4,3,0,2,1:T(8,128)(2,1)}, bf16[2,2,2,64,256]{4,3,0,2,1:T(8,128)(2,1)S(1)}, u32[]{:S(2)}, u32[]{:S(2)}) collective-permute-start(bf16[2,2,2,64,256]{4,3,0,2,1:T(8,128)(2,1)} %fusion.89), channel_id=1, source_target_pairs={{0,254},{2,0},{4,2},{6,4},{8,6},{10,8},{12,10},{14,12},{16,14},{18... | collective-permute-start | bytes 786440 | tf_op jit(solution)/shard_map/ppermute | solution.py:22
  469.3 20.3 %collective-permute-start.11 = (bf16[2,2,2,64,256]{4,3,0,2,1:T(8,128)(2,1)}, bf16[2,2,2,64,256]{4,3,0,2,1:T(8,128)(2,1)S(1)}, u32[]{:S(2)}, u32[]{:S(2)}) collective-permute-start(bf16[2,2,2,64,256]{4,3,0,2,1:T(8,128)(2,1)} %collective-permute-done.8), channel_id=1, source_target_pairs={{0,2},{2,4},{4,6},{6,8},{8,10},{10,12},{12,14},{14,16},{16,18},{18... | collective-permute-start | bytes 786440 | tf_op jit(solution)/shard_map/ppermute | solution.py:22
  484.3 17.6 %collective-permute-start.17 = (bf16[2,2,2,64,256]{4,3,0,2,1:T(8,128)(2,1)S(1)}, bf16[2,2,2,64,256]{4,3,0,2,1:T(8,128)(2,1)S(1)}, u32[]{:S(2)}, u32[]{:S(2)}) collective-permute-start(bf16[2,2,2,64,256]{4,3,0,2,1:T(8,128)(2,1)S(1)} %collective-permute-done.14), channel_id=1, source_target_pairs={{0,254},{2,0},{4,2},{6,4},{8,6},{10,8},{12,10},{14,12},{16,14},{18... | collective-permute-start | bytes 786440 | tf_op jit(solution)/shard_map/ppermute | solution.py:22
  504.2 11.0 %copy-start.19 = (f32[2,256,512]{2,1,0:T(8,128)S(1)}, f32[2,256,512]{2,1,0:T(8,128)}, u32[]{:S(2)}) copy-start(f32[2,256,512]{2,1,0:T(8,128)} %copy.99) | copy-start | bytes 3145732
  506.6 8.6 %copy-start.16 = (f32[2,256,512]{2,1,0:T(8,128)S(1)}, f32[2,256,512]{2,1,0:T(8,128)}, u32[]{:S(2)}) copy-start(f32[2,256,512]{2,1,0:T(8,128)} %copy.93) | copy-start | bytes 3145732
  506.7 8.6 %copy-start.17 = (f32[2,256,512]{2,1,0:T(8,128)S(1)}, f32[2,256,512]{2,1,0:T(8,128)}, u32[]{:S(2)}) copy-start(f32[2,256,512]{2,1,0:T(8,128)} %copy.95) | copy-start | bytes 3145732
  506.7 8.6 %copy-start.18 = (f32[2,256,512]{2,1,0:T(8,128)S(1)}, f32[2,256,512]{2,1,0:T(8,128)}, u32[]{:S(2)}) copy-start(f32[2,256,512]{2,1,0:T(8,128)} %copy.96) | copy-start | bytes 3145732
  508.2 7.1 %copy-start.14 = (f32[2,256,512]{2,1,0:T(8,128)S(1)}, f32[2,256,512]{2,1,0:T(8,128)}, u32[]{:S(2)}) copy-start(f32[2,256,512]{2,1,0:T(8,128)} %copy.124) | copy-start | bytes 3145732
  508.2 7.1 %copy-start.15 = (f32[2,256,512]{2,1,0:T(8,128)S(1)}, f32[2,256,512]{2,1,0:T(8,128)}, u32[]{:S(2)}) copy-start(f32[2,256,512]{2,1,0:T(8,128)} %copy.92) | copy-start | bytes 3145732
  538.7 60.3 %copy-start.58 = (f32[2,64,128]{2,1,0:T(8,128)S(1)}, f32[2,64,128]{2,1,0:T(8,128)}, u32[]{:S(2)}) copy-start(f32[2,64,128]{2,1,0:T(8,128)} %param.11) | copy-start | bytes 196612
  539.4 146.9 %copy-start.1 = (f32[512,256]{1,0:T(8,128)S(1)}, f32[512,256]{1,0:T(8,128)}, u32[]{:S(2)}) copy-start(f32[512,256]{1,0:T(8,128)} %param.13) | copy-start | bytes 1572868
  599.9 7.1 %collective-permute-start.20 = (bf16[2,2,2,64,128]{4,3,0,2,1:T(8,128)(2,1)S(1)}, bf16[2,2,2,64,128]{4,3,0,2,1:T(8,128)(2,1)S(1)}, u32[]{:S(2)}, u32[]{:S(2)}) collective-permute-start(bf16[2,2,2,64,128]{4,3,0,2,1:T(8,128)(2,1)S(1)} %add_convert_fusion.7), channel_id=1, source_target_pairs={{0,256},{256,0},{1,257},{257,1},{2,258},{258,2},{3,259},{259,3},{4... | collective-permute-start | bytes 393224 | tf_op jit(solution)/shard_map/ppermute | solution.py:17
  607.1 3.2 collective-permute-start.21
  610.3 7.4 %collective-permute-start.22 = (bf16[2,2,2,64,128]{4,3,0,2,1:T(8,128)(2,1)S(1)}, bf16[2,2,2,64,128]{4,3,0,2,1:T(8,128)(2,1)S(1)}, u32[]{:S(2)}, u32[]{:S(2)}) collective-permute-start(bf16[2,2,2,64,128]{4,3,0,2,1:T(8,128)(2,1)S(1)} %collective-permute-done.21), channel_id=1, source_target_pairs={{0,4},{4,0},{2,6},{6,2},{8,12},{12,8},{10,14},{14,10},{16,20},{20,... | collective-permute-start | bytes 393224 | tf_op jit(solution)/shard_map/ppermute | solution.py:17
  617.7 10.3 %collective-permute-start.23 = (bf16[2,2,2,64,128]{4,3,0,2,1:T(8,128)(2,1)S(1)}, bf16[2,2,2,64,128]{4,3,0,2,1:T(8,128)(2,1)S(1)}, u32[]{:S(2)}, u32[]{:S(2)}) collective-permute-start(bf16[2,2,2,64,128]{4,3,0,2,1:T(8,128)(2,1)S(1)} %collective-permute-done.22), channel_id=1, source_target_pairs={{0,8},{8,0},{2,10},{10,2},{4,12},{12,4},{6,14},{14,6},{16,24},{24,... | collective-permute-start | bytes 393224 | tf_op jit(solution)/shard_map/ppermute | solution.py:17
  628.1 17.5 %collective-permute-start.24 = (bf16[2,2,2,64,128]{4,3,0,2,1:T(8,128)(2,1)S(1)}, bf16[2,2,2,64,128]{4,3,0,2,1:T(8,128)(2,1)S(1)}, u32[]{:S(2)}, u32[]{:S(2)}) collective-permute-start(bf16[2,2,2,64,128]{4,3,0,2,1:T(8,128)(2,1)S(1)} %collective-permute-done.23), channel_id=1, source_target_pairs={{0,16},{16,0},{2,18},{18,2},{4,20},{20,4},{6,22},{22,6},{8,24},{24... | collective-permute-start | bytes 393224 | tf_op jit(solution)/shard_map/ppermute | solution.py:17
  645.6 24.1 %collective-permute-start.25 = (bf16[2,2,2,64,128]{4,3,0,2,1:T(8,128)(2,1)S(1)}, bf16[2,2,2,64,128]{4,3,0,2,1:T(8,128)(2,1)S(1)}, u32[]{:S(2)}, u32[]{:S(2)}) collective-permute-start(bf16[2,2,2,64,128]{4,3,0,2,1:T(8,128)(2,1)S(1)} %collective-permute-done.24), channel_id=1, source_target_pairs={{0,32},{32,0},{2,34},{34,2},{4,36},{36,4},{6,38},{38,6},{8,40},{40... | collective-permute-start | bytes 393224 | tf_op jit(solution)/shard_map/ppermute | solution.py:17
  669.7 6.8 collective-permute-start.26
  676.5 8.4 %collective-permute-start.27 = (bf16[2,2,2,64,128]{4,3,0,2,1:T(8,128)(2,1)S(1)}, bf16[2,2,2,64,128]{4,3,0,2,1:T(8,128)(2,1)S(1)}, u32[]{:S(2)}, u32[]{:S(2)}) collective-permute-start(bf16[2,2,2,64,128]{4,3,0,2,1:T(8,128)(2,1)S(1)} %collective-permute-done.26), channel_id=1, source_target_pairs={{0,128},{128,0},{2,130},{130,2},{4,132},{132,4},{6,134},{134,6},{8... | collective-permute-start | bytes 393224 | tf_op jit(solution)/shard_map/ppermute | solution.py:17
  (41 other events, 124.5 us)
Sparse Core Ops, SparseCore 0:
  540.6 57.0 reduce-scatter.3
